TPU v7x, 512 devices: a whole 4x8x8 slice. The times are simulated.
512 devices in a mesh: grp: 64 (over y, x, core), batch: 8 (over z).
Axes of the slice: x: 4, y: 8, z: 8, core: 2. Of those that a mesh axis runs over, the one named last changes fastest.
Arguments:
- tokens: bfloat16 [512, 8, 16384], P('batch', None, 'grp'), may hold values from -6 to 6
- input_weights: bfloat16 [2, 1024, 65536], P(None, 'batch', 'grp'), may hold values from -0.1875 to 0.1875
- recur_weights: bfloat16 [2, 1024, 65536], P(None, 'batch', 'grp'), may hold values from -0.1875 to 0.1875
- biases: float32 [2, 65536], P(None, 'grp'), may hold values from -1 to 4
- shuffle: int32 [16384], replicated, may hold values from 0 to 16383, as said below
Outputs:
- second_states: bfloat16 [512, 8, 16384], P('batch', None, 'grp')
Inputs may be any that keep to these rules, and one draw needn't show every extreme that they name: shuffle is a permutation of the 16384 channels. Position j * 256 + s * 4 + k (k below 4) holds a channel of block s, that is one in [s * 256, (s + 1) * 256).
All inputs are finite; a program needn't handle non-finite values.
Results may differ from a plain program's by a relative error of at most 0.0034.
Values may be sent and summed in bfloat16 or wider, within the bound.
A program may use at most 64 MiB of HBM per device.

v0:
```python
import jax
import jax.numpy as jnp
from jax import lax
from jax.sharding import PartitionSpec as P


def partner(array, axis, distance):
    return lax.ppermute(array, axis, [(i, i ^ 1 << distance) for i in range(lax.axis_size(axis))])


def order_pair(mine, other, level):
    position = lax.axis_index("grp")
    lower = position >> level & 1 == 0
    return jnp.where(
        lower, jnp.concatenate([mine, other], axis=-1), jnp.concatenate([other, mine], axis=-1)
    )


def inputs_group(piece, levels):
    for level in range(levels):
        other = partner(piece, "grp", level)
        piece = order_pair(piece, other, level)
    return piece


def state_group(piece, levels):
    for level in range(levels):
        other = partner(piece, "grp", level)
        piece = order_pair(piece, other, level)
    return piece


def layer_rows(input_weights, recur_weights, layer):
    return (
        lax.all_gather(input_weights[layer], "batch", axis=0, tiled=True),
        lax.all_gather(recur_weights[layer], "batch", axis=0, tiled=True),
    )


def run_block(inputs, w_in, w_rec, bias, levels):
    seqs, steps, width = inputs.shape
    unit_count = w_in.shape[1] // 4
    proj = jnp.dot(
        inputs.reshape(seqs * steps, width), w_in, preferred_element_type=jnp.float32
    ).reshape(seqs, steps, 4 * unit_count)
    state = jnp.zeros((seqs, unit_count), jnp.bfloat16)
    cell = jnp.zeros((seqs, unit_count), jnp.float32)
    outputs = []
    for step in range(steps):
        if step == 0:
            whole = jnp.zeros((seqs, width), jnp.bfloat16)
        else:
            whole = state_group(state, levels)
        pre = proj[:, step] + jnp.dot(whole, w_rec, preferred_element_type=jnp.float32) + bias
        ingate = jax.nn.sigmoid(pre[:, 0:unit_count])
        forget = jax.nn.sigmoid(pre[:, unit_count : 2 * unit_count])
        cellgate = jnp.tanh(pre[:, 2 * unit_count : 3 * unit_count])
        outgate = jax.nn.sigmoid(pre[:, 3 * unit_count :])
        cell = forget * cell + ingate * cellgate
        state = (outgate * jnp.tanh(cell)).astype(jnp.bfloat16)
        outputs.append(state)
    return jnp.stack(outputs, axis=1)


def local(tokens, input_weights, recur_weights, biases, shuffle):
    devices = lax.axis_size("grp")
    position = lax.axis_index("grp")
    unit_count = tokens.shape[2]
    width = input_weights.shape[1] * lax.axis_size("batch")
    split = width // unit_count
    levels = split.bit_length() - 1
    kslot = unit_count // devices
    first_in, first_rec = layer_rows(input_weights, recur_weights, 0)
    first_inputs = inputs_group(tokens, levels)
    first = run_block(first_inputs, first_in, first_rec, biases[0], levels)
    table = shuffle.reshape(devices, devices, kslot)
    picked = (
        lax.dynamic_index_in_dim(table, position, axis=1, keepdims=False) - position * unit_count
    )
    outgoing = jnp.take(first, picked.reshape(-1), axis=2)
    mixed = lax.all_to_all(outgoing, "grp", split_axis=2, concat_axis=2, tiled=True)
    second_inputs = inputs_group(mixed, levels)
    second_in, second_rec = layer_rows(input_weights, recur_weights, 1)
    return run_block(second_inputs, second_in, second_rec, biases[1], levels)


def solution(mesh):
    return jax.shard_map(
        local,
        mesh=mesh,
        in_specs=(
            P("batch", None, "grp"),
            P(None, "batch", "grp"),
            P(None, "batch", "grp"),
            P(None, "grp"),
            P(),
        ),
        out_specs=P("batch", None, "grp"),
        check_vma=False,
    )
```

profile of v0, /device:TPU:1, one launch (start us, length us, event | category | flops | bytes accessed | tf_op | source)
XLA Modules:
  0.0 310.0 jit_solution(17923178078882372201)
XLA Ops:
  11.0 8.8 %collective-permute-start = (bf16[64,8,256]{0,1,2:T(8,128)(2,1)S(1)}, bf16[64,8,256]{0,1,2:T(8,128)(2,1)S(1)}, u32[]{:S(2)}, u32[]{:S(2)}) collective-permute-start(bf16[64,8,256]{0,1,2:T(8,128)(2,1)S(1)} %copy.50), channel_id=1, source_target_pairs={{0,8},{8,0},{16,24},{24,16},{32,40},{40,32},{48,56},{56,48},{64,72... | collective-permute-start | bytes 786440 | tf_op jit(solution)/shard_map/ppermute | solution.py:8
  25.0 13.1 %collective-permute-done.1 = bf16[64,8,512]{2,1,0:T(8,128)(2,1)S(1)} collective-permute-done((bf16[64,8,512]{2,1,0:T(8,128)(2,1)S(1)}, bf16[64,8,512]{2,1,0:T(8,128)(2,1)S(1)}, u32[]{:S(2)}, u32[]{:S(2)}) %collective-permute-start.1) | collective-permute-done | bytes 524320 | tf_op jit(solution)/shard_map/ppermute | solution.py:8
  45.1 10.4 %all-gather.9.cloned.1.call-done = bf16[1,1024,1024]{2,1,0:T(8,128)(2,1)} async-done(((bf16[1,128,1024]{2,1,0:T(8,128)(2,1)}), bf16[1,1024,1024]{2,1,0:T(8,128)(2,1)}) %all-gather.9.cloned.1.call-update) | async-done | bytes 2097168 | tf_op jit(solution)/shard_map/all_gather | solution.py:35
  55.5 2.8 fusion.35
  60.6 39.8 %all-gather.11.cloned.1.call-done = bf16[1,1024,1024]{2,1,0:T(8,128)(2,1)} async-done(((bf16[1,128,1024]{2,1,0:T(8,128)(2,1)}), bf16[1,1024,1024]{2,1,0:T(8,128)(2,1)}) %all-gather.11.cloned.1.call-update) | async-done | bytes 2097168 | tf_op jit(solution)/shard_map/all_gather | solution.py:36
  102.7 6.6 %collective-permute-start.2 = (bf16[64,256]{1,0:T(8,128)(2,1)S(1)}, bf16[64,256]{1,0:T(8,128)(2,1)S(1)}, u32[]{:S(2)}, u32[]{:S(2)}) collective-permute-start(bf16[64,256]{1,0:T(8,128)(2,1)S(1)} %get-tuple-element.47), channel_id=1, source_target_pairs={{0,8},{8,0},{16,24},{24,16},{32,40},{40,32},{48,56},{56,48},{64,72... | collective-permute-start | bytes 98312 | tf_op jit(solution)/shard_map/ppermute | solution.py:8
  110.2 3.1 collective-permute-start.3
  115.8 3.4 %collective-permute-start.4 = (bf16[64,256]{1,0:T(8,128)(2,1)S(1)}, bf16[64,256]{1,0:T(8,128)(2,1)S(1)}, u32[]{:S(2)}, u32[]{:S(2)}) collective-permute-start(bf16[64,256]{1,0:T(8,128)(2,1)S(1)} %get-tuple-element.44), channel_id=1, source_target_pairs={{0,8},{8,0},{16,24},{24,16},{32,40},{40,32},{48,56},{56,48},{64,72... | collective-permute-start | bytes 98312 | tf_op jit(solution)/shard_map/ppermute | solution.py:8
  120.1 3.1 collective-permute-start.5
  126.1 3.0 collective-permute-start.6
  130.0 3.1 collective-permute-start.7
  136.0 3.0 collective-permute-start.8
  139.8 3.1 collective-permute-start.9
  146.5 3.0 collective-permute-start.10
  150.4 3.3 %collective-permute-start.11 = (bf16[64,512]{1,0:T(8,128)(2,1)S(1)}, bf16[64,512]{1,0:T(8,128)(2,1)S(1)}, u32[]{:S(2)}, u32[]{:S(2)}) collective-permute-start(bf16[64,512]{1,0:T(8,128)(2,1)S(1)} %maximum_select_fusion.50), channel_id=1, source_target_pairs={{0,16},{8,24},{16,0},{24,8},{32,48},{40,56},{48,32},{56,40},{64,80... | collective-permute-start | bytes 196616 | tf_op jit(solution)/shard_map/ppermute | solution.py:8
  153.7 3.5 %reshape.64 = s32[64,64,4]{2,1,0:T(8,128)} reshape(s32[16384]{0:T(1024)S(1)} %copy-done.7) | data formatting | bytes 131072 | tf_op jit(solution)/shard_map/reshape | solution.py:76
  165.1 3.3 %collective-permute-done.13 = bf16[64,512]{1,0:T(8,128)(2,1)S(1)} collective-permute-done((bf16[64,512]{1,0:T(8,128)(2,1)S(1)}, bf16[64,512]{1,0:T(8,128)(2,1)S(1)}, u32[]{:S(2)}, u32[]{:S(2)}) %collective-permute-start.13) | collective-permute-done | bytes 65568 | tf_op jit(solution)/shard_map/ppermute | solution.py:8
  169.0 2.7 collective-permute-start.14
  174.7 3.2 %collective-permute-done.15 = bf16[64,512]{1,0:T(8,128)(2,1)S(1)} collective-permute-done((bf16[64,512]{1,0:T(8,128)(2,1)S(1)}, bf16[64,512]{1,0:T(8,128)(2,1)S(1)}, u32[]{:S(2)}, u32[]{:S(2)}) %collective-permute-start.15) | collective-permute-done | bytes 65568 | tf_op jit(solution)/shard_map/ppermute | solution.py:8
  180.3 23.5 %all_to_all.5 = bf16[64,2,1024]{2,1,0:T(2,128)(2,1)S(1)} all-to-all(bf16[64,2,1024]{2,1,0:T(2,128)(2,1)S(1)} %reshape.91), channel_id=1, replica_groups=mesh['grp'=64,'batch'=8] {'grp'}, dimensions={0} | all-to-all | bytes 524288 | tf_op jit(solution)/shard_map/all_to_all | solution.py:81
  212.0 12.8 %collective-permute-done.17 = bf16[64,8,512]{2,1,0:T(8,128)(2,1)S(1)} collective-permute-done((bf16[64,8,512]{2,1,0:T(8,128)(2,1)S(1)}, bf16[64,8,512]{2,1,0:T(8,128)(2,1)S(1)}, u32[]{:S(2)}, u32[]{:S(2)}) %collective-permute-start.17) | collective-permute-done | bytes 524320 | tf_op jit(solution)/shard_map/ppermute | solution.py:8
  228.1 3.5 %fusion.16 = f32[64,8,1024]{2,0,1:T(8,128)S(1)} fusion(bf16[1,1024,1024]{2,1,0:T(8,128)(2,1)} %all-gather.13.cloned.1.call-done, bf16[64,8,1024]{0,1,2:T(8,128)(2,1)} %maximum_select_fusion.1), kind=kOutput, calls=%fused_computation.19 | convolution fusion | flops 1073741824 | bytes 5242880 | tf_op jit(solution)/shard_map/dot_general | solution.py:43
  234.0 3.0 collective-permute-start.18
  240.2 2.7 collective-permute-done.19
  243.4 3.4 %collective-permute-start.20 = (bf16[64,256]{1,0:T(8,128)(2,1)S(1)}, bf16[64,256]{1,0:T(8,128)(2,1)S(1)}, u32[]{:S(2)}, u32[]{:S(2)}) collective-permute-start(bf16[64,256]{1,0:T(8,128)(2,1)S(1)} %get-tuple-element.21), channel_id=1, source_target_pairs={{0,8},{8,0},{16,24},{24,16},{32,40},{40,32},{48,56},{56,48},{64,72... | collective-permute-start | bytes 98312 | tf_op jit(solution)/shard_map/ppermute | solution.py:8
  250.1 2.7 collective-permute-done.21
  253.3 3.4 %collective-permute-start.22 = (bf16[64,256]{1,0:T(8,128)(2,1)S(1)}, bf16[64,256]{1,0:T(8,128)(2,1)S(1)}, u32[]{:S(2)}, u32[]{:S(2)}) collective-permute-start(bf16[64,256]{1,0:T(8,128)(2,1)S(1)} %get-tuple-element.18), channel_id=1, source_target_pairs={{0,8},{8,0},{16,24},{24,16},{32,40},{40,32},{48,56},{56,48},{64,72... | collective-permute-start | bytes 98312 | tf_op jit(solution)/shard_map/ppermute | solution.py:8
  263.2 3.4 %collective-permute-start.24 = (bf16[64,256]{1,0:T(8,128)(2,1)S(1)}, bf16[64,256]{1,0:T(8,128)(2,1)S(1)}, u32[]{:S(2)}, u32[]{:S(2)}) collective-permute-start(bf16[64,256]{1,0:T(8,128)(2,1)S(1)} %get-tuple-element.15), channel_id=1, source_target_pairs={{0,8},{8,0},{16,24},{24,16},{32,40},{40,32},{48,56},{56,48},{64,72... | collective-permute-start | bytes 98312 | tf_op jit(solution)/shard_map/ppermute | solution.py:8
  269.8 2.7 collective-permute-done.25
  273.0 3.4 %collective-permute-start.26 = (bf16[64,256]{1,0:T(8,128)(2,1)S(1)}, bf16[64,256]{1,0:T(8,128)(2,1)S(1)}, u32[]{:S(2)}, u32[]{:S(2)}) collective-permute-start(bf16[64,256]{1,0:T(8,128)(2,1)S(1)} %get-tuple-element.12), channel_id=1, source_target_pairs={{0,8},{8,0},{16,24},{24,16},{32,40},{40,32},{48,56},{56,48},{64,72... | collective-permute-start | bytes 98312 | tf_op jit(solution)/shard_map/ppermute | solution.py:8
  282.9 3.4 %collective-permute-start.28 = (bf16[64,256]{1,0:T(8,128)(2,1)S(1)}, bf16[64,256]{1,0:T(8,128)(2,1)S(1)}, u32[]{:S(2)}, u32[]{:S(2)}) collective-permute-start(bf16[64,256]{1,0:T(8,128)(2,1)S(1)} %get-tuple-element.9), channel_id=1, source_target_pairs={{0,8},{8,0},{16,24},{24,16},{32,40},{40,32},{48,56},{56,48},{64,72... | collective-permute-start | bytes 98312 | tf_op jit(solution)/shard_map/ppermute | solution.py:8
  292.7 3.4 %collective-permute-start.30 = (bf16[64,256]{1,0:T(8,128)(2,1)S(1)}, bf16[64,256]{1,0:T(8,128)(2,1)S(1)}, u32[]{:S(2)}, u32[]{:S(2)}) collective-permute-start(bf16[64,256]{1,0:T(8,128)(2,1)S(1)} %get-tuple-element.6), channel_id=1, source_target_pairs={{0,8},{8,0},{16,24},{24,16},{32,40},{40,32},{48,56},{56,48},{64,72... | collective-permute-start | bytes 98312 | tf_op jit(solution)/shard_map/ppermute | solution.py:8
  (139 shorter events, 102.4 us)
Async XLA Ops:
  6.5 49.0 %all-gather.9.cloned.1.call-start = ((), (), s32[]{:S(2)}) async-start(), calls=%async_computation.1 | async-start | bytes 2359296 | tf_op jit(solution)/shard_map/all_gather | solution.py:35
  8.5 91.9 %all-gather.11.cloned.1.call-start = ((), (), s32[]{:S(2)}) async-start(), calls=%async_computation.2 | async-start | bytes 2359296 | tf_op jit(solution)/shard_map/all_gather | solution.py:36
  10.5 217.7 %all-gather.13.cloned.1.call-start = ((), (), s32[]{:S(2)}) async-start(), calls=%async_computation.3 | async-start | bytes 2359296 | tf_op jit(solution)/shard_map/all_gather | solution.py:35
  11.0 10.3 %collective-permute-start = (bf16[64,8,256]{0,1,2:T(8,128)(2,1)S(1)}, bf16[64,8,256]{0,1,2:T(8,128)(2,1)S(1)}, u32[]{:S(2)}, u32[]{:S(2)}) collective-permute-start(bf16[64,8,256]{0,1,2:T(8,128)(2,1)S(1)} %copy.50), channel_id=1, source_target_pairs={{0,8},{8,0},{16,24},{24,16},{32,40},{40,32},{48,56},{56,48},{64,72... | collective-permute-start | bytes 786440 | tf_op jit(solution)/shard_map/ppermute | solution.py:8
  23.0 15.1 %collective-permute-start.1 = (bf16[64,8,512]{2,1,0:T(8,128)(2,1)S(1)}, bf16[64,8,512]{2,1,0:T(8,128)(2,1)S(1)}, u32[]{:S(2)}, u32[]{:S(2)}) collective-permute-start(bf16[64,8,512]{2,1,0:T(8,128)(2,1)S(1)} %copy.52), channel_id=1, source_target_pairs={{0,16},{8,24},{16,0},{24,8},{32,48},{40,56},{48,32},{56,40},{64,80... | collective-permute-start | bytes 1572872 | tf_op jit(solution)/shard_map/ppermute | solution.py:8
  24.9 206.7 %all-gather.15.cloned.1.call-start = ((), (), s32[]{:S(2)}) async-start(), calls=%async_computation.4 | async-start | bytes 2359296 | tf_op jit(solution)/shard_map/all_gather | solution.py:36
  102.7 7.5 %collective-permute-start.2 = (bf16[64,256]{1,0:T(8,128)(2,1)S(1)}, bf16[64,256]{1,0:T(8,128)(2,1)S(1)}, u32[]{:S(2)}, u32[]{:S(2)}) collective-permute-start(bf16[64,256]{1,0:T(8,128)(2,1)S(1)} %get-tuple-element.47), channel_id=1, source_target_pairs={{0,8},{8,0},{16,24},{24,16},{32,40},{40,32},{48,56},{56,48},{64,72... | collective-permute-start | bytes 98312 | tf_op jit(solution)/shard_map/ppermute | solution.py:8
  110.2 5.0 %collective-permute-start.3 = (bf16[64,512]{1,0:T(8,128)(2,1)S(1)}, bf16[64,512]{1,0:T(8,128)(2,1)S(1)}, u32[]{:S(2)}, u32[]{:S(2)}) collective-permute-start(bf16[64,512]{1,0:T(8,128)(2,1)S(1)} %maximum_select_fusion.46), channel_id=1, source_target_pairs={{0,16},{8,24},{16,0},{24,8},{32,48},{40,56},{48,32},{56,40},{64,80... | collective-permute-start | bytes 196616 | tf_op jit(solution)/shard_map/ppermute | solution.py:8
  115.8 4.3 %collective-permute-start.4 = (bf16[64,256]{1,0:T(8,128)(2,1)S(1)}, bf16[64,256]{1,0:T(8,128)(2,1)S(1)}, u32[]{:S(2)}, u32[]{:S(2)}) collective-permute-start(bf16[64,256]{1,0:T(8,128)(2,1)S(1)} %get-tuple-element.44), channel_id=1, source_target_pairs={{0,8},{8,0},{16,24},{24,16},{32,40},{40,32},{48,56},{56,48},{64,72... | collective-permute-start | bytes 98312 | tf_op jit(solution)/shard_map/ppermute | solution.py:8
  120.1 5.4 %collective-permute-start.5 = (bf16[64,512]{1,0:T(8,128)(2,1)S(1)}, bf16[64,512]{1,0:T(8,128)(2,1)S(1)}, u32[]{:S(2)}, u32[]{:S(2)}) collective-permute-start(bf16[64,512]{1,0:T(8,128)(2,1)S(1)} %maximum_select_fusion.47), channel_id=1, source_target_pairs={{0,16},{8,24},{16,0},{24,8},{32,48},{40,56},{48,32},{56,40},{64,80... | collective-permute-start | bytes 196616 | tf_op jit(solution)/shard_map/ppermute | solution.py:8
  126.1 3.9 %collective-permute-start.6 = (bf16[64,256]{1,0:T(8,128)(2,1)S(1)}, bf16[64,256]{1,0:T(8,128)(2,1)S(1)}, u32[]{:S(2)}, u32[]{:S(2)}) collective-permute-start(bf16[64,256]{1,0:T(8,128)(2,1)S(1)} %get-tuple-element.41), channel_id=1, source_target_pairs={{0,8},{8,0},{16,24},{24,16},{32,40},{40,32},{48,56},{56,48},{64,72... | collective-permute-start | bytes 98312 | tf_op jit(solution)/shard_map/ppermute | solution.py:8
  130.0 5.4 %collective-permute-start.7 = (bf16[64,512]{1,0:T(8,128)(2,1)S(1)}, bf16[64,512]{1,0:T(8,128)(2,1)S(1)}, u32[]{:S(2)}, u32[]{:S(2)}) collective-permute-start(bf16[64,512]{1,0:T(8,128)(2,1)S(1)} %maximum_select_fusion.48), channel_id=1, source_target_pairs={{0,16},{8,24},{16,0},{24,8},{32,48},{40,56},{48,32},{56,40},{64,80... | collective-permute-start | bytes 196616 | tf_op jit(solution)/shard_map/ppermute | solution.py:8
  136.0 3.9 %collective-permute-start.8 = (bf16[64,256]{1,0:T(8,128)(2,1)S(1)}, bf16[64,256]{1,0:T(8,128)(2,1)S(1)}, u32[]{:S(2)}, u32[]{:S(2)}) collective-permute-start(bf16[64,256]{1,0:T(8,128)(2,1)S(1)} %get-tuple-element.38), channel_id=1, source_target_pairs={{0,8},{8,0},{16,24},{24,16},{32,40},{40,32},{48,56},{56,48},{64,72... | collective-permute-start | bytes 98312 | tf_op jit(solution)/shard_map/ppermute | solution.py:8
  139.8 5.4 %collective-permute-start.9 = (bf16[64,512]{1,0:T(8,128)(2,1)S(1)}, bf16[64,512]{1,0:T(8,128)(2,1)S(1)}, u32[]{:S(2)}, u32[]{:S(2)}) collective-permute-start(bf16[64,512]{1,0:T(8,128)(2,1)S(1)} %maximum_select_fusion.49), channel_id=1, source_target_pairs={{0,16},{8,24},{16,0},{24,8},{32,48},{40,56},{48,32},{56,40},{64,80... | collective-permute-start | bytes 196616 | tf_op jit(solution)/shard_map/ppermute | solution.py:8
  150.4 6.9 %collective-permute-start.11 = (bf16[64,512]{1,0:T(8,128)(2,1)S(1)}, bf16[64,512]{1,0:T(8,128)(2,1)S(1)}, u32[]{:S(2)}, u32[]{:S(2)}) collective-permute-start(bf16[64,512]{1,0:T(8,128)(2,1)S(1)} %maximum_select_fusion.50), channel_id=1, source_target_pairs={{0,16},{8,24},{16,0},{24,8},{32,48},{40,56},{48,32},{56,40},{64,80... | collective-permute-start | bytes 196616 | tf_op jit(solution)/shard_map/ppermute | solution.py:8
  157.9 4.9 %collective-permute-start.12 = (bf16[64,256]{1,0:T(8,128)(2,1)S(1)}, bf16[64,256]{1,0:T(8,128)(2,1)S(1)}, u32[]{:S(2)}, u32[]{:S(2)}) collective-permute-start(bf16[64,256]{1,0:T(8,128)(2,1)S(1)} %get-tuple-element.32), channel_id=1, source_target_pairs={{0,8},{8,0},{16,24},{24,16},{32,40},{40,32},{48,56},{56,48},{64,72... | collective-permute-start | bytes 98312 | tf_op jit(solution)/shard_map/ppermute | solution.py:8
  162.8 5.6 %collective-permute-start.13 = (bf16[64,512]{1,0:T(8,128)(2,1)S(1)}, bf16[64,512]{1,0:T(8,128)(2,1)S(1)}, u32[]{:S(2)}, u32[]{:S(2)}) collective-permute-start(bf16[64,512]{1,0:T(8,128)(2,1)S(1)} %maximum_select_fusion.51), channel_id=1, source_target_pairs={{0,16},{8,24},{16,0},{24,8},{32,48},{40,56},{48,32},{56,40},{64,80... | collective-permute-start | bytes 196616 | tf_op jit(solution)/shard_map/ppermute | solution.py:8
  172.5 5.4 %collective-permute-start.15 = (bf16[64,512]{1,0:T(8,128)(2,1)S(1)}, bf16[64,512]{1,0:T(8,128)(2,1)S(1)}, u32[]{:S(2)}, u32[]{:S(2)}) collective-permute-start(bf16[64,512]{1,0:T(8,128)(2,1)S(1)} %maximum_select_fusion.52), channel_id=1, source_target_pairs={{0,16},{8,24},{16,0},{24,8},{32,48},{40,56},{48,32},{56,40},{64,80... | collective-permute-start | bytes 196616 | tf_op jit(solution)/shard_map/ppermute | solution.py:8
  209.6 15.2 %collective-permute-start.17 = (bf16[64,8,512]{2,1,0:T(8,128)(2,1)S(1)}, bf16[64,8,512]{2,1,0:T(8,128)(2,1)S(1)}, u32[]{:S(2)}, u32[]{:S(2)}) collective-permute-start(bf16[64,8,512]{2,1,0:T(8,128)(2,1)S(1)} %copy.64), channel_id=1, source_target_pairs={{0,16},{8,24},{16,0},{24,8},{32,48},{40,56},{48,32},{56,40},{64,80... | collective-permute-start | bytes 1572872 | tf_op jit(solution)/shard_map/ppermute | solution.py:8
  237.8 5.0 %collective-permute-start.19 = (bf16[64,512]{1,0:T(8,128)(2,1)S(1)}, bf16[64,512]{1,0:T(8,128)(2,1)S(1)}, u32[]{:S(2)}, u32[]{:S(2)}) collective-permute-start(bf16[64,512]{1,0:T(8,128)(2,1)S(1)} %maximum_select_fusion.53), channel_id=1, source_target_pairs={{0,16},{8,24},{16,0},{24,8},{32,48},{40,56},{48,32},{56,40},{64,80... | collective-permute-start | bytes 196616 | tf_op jit(solution)/shard_map/ppermute | solution.py:8
  243.4 4.3 %collective-permute-start.20 = (bf16[64,256]{1,0:T(8,128)(2,1)S(1)}, bf16[64,256]{1,0:T(8,128)(2,1)S(1)}, u32[]{:S(2)}, u32[]{:S(2)}) collective-permute-start(bf16[64,256]{1,0:T(8,128)(2,1)S(1)} %get-tuple-element.21), channel_id=1, source_target_pairs={{0,8},{8,0},{16,24},{24,16},{32,40},{40,32},{48,56},{56,48},{64,72... | collective-permute-start | bytes 98312 | tf_op jit(solution)/shard_map/ppermute | solution.py:8
  247.7 5.0 %collective-permute-start.21 = (bf16[64,512]{1,0:T(8,128)(2,1)S(1)}, bf16[64,512]{1,0:T(8,128)(2,1)S(1)}, u32[]{:S(2)}, u32[]{:S(2)}) collective-permute-start(bf16[64,512]{1,0:T(8,128)(2,1)S(1)} %maximum_select_fusion.54), channel_id=1, source_target_pairs={{0,16},{8,24},{16,0},{24,8},{32,48},{40,56},{48,32},{56,40},{64,80... | collective-permute-start | bytes 196616 | tf_op jit(solution)/shard_map/ppermute | solution.py:8
  253.3 4.3 %collective-permute-start.22 = (bf16[64,256]{1,0:T(8,128)(2,1)S(1)}, bf16[64,256]{1,0:T(8,128)(2,1)S(1)}, u32[]{:S(2)}, u32[]{:S(2)}) collective-permute-start(bf16[64,256]{1,0:T(8,128)(2,1)S(1)} %get-tuple-element.18), channel_id=1, source_target_pairs={{0,8},{8,0},{16,24},{24,16},{32,40},{40,32},{48,56},{56,48},{64,72... | collective-permute-start | bytes 98312 | tf_op jit(solution)/shard_map/ppermute | solution.py:8
  257.6 5.0 %collective-permute-start.23 = (bf16[64,512]{1,0:T(8,128)(2,1)S(1)}, bf16[64,512]{1,0:T(8,128)(2,1)S(1)}, u32[]{:S(2)}, u32[]{:S(2)}) collective-permute-start(bf16[64,512]{1,0:T(8,128)(2,1)S(1)} %maximum_select_fusion.55), channel_id=1, source_target_pairs={{0,16},{8,24},{16,0},{24,8},{32,48},{40,56},{48,32},{56,40},{64,80... | collective-permute-start | bytes 196616 | tf_op jit(solution)/shard_map/ppermute | solution.py:8
  263.2 4.3 %collective-permute-start.24 = (bf16[64,256]{1,0:T(8,128)(2,1)S(1)}, bf16[64,256]{1,0:T(8,128)(2,1)S(1)}, u32[]{:S(2)}, u32[]{:S(2)}) collective-permute-start(bf16[64,256]{1,0:T(8,128)(2,1)S(1)} %get-tuple-element.15), channel_id=1, source_target_pairs={{0,8},{8,0},{16,24},{24,16},{32,40},{40,32},{48,56},{56,48},{64,72... | collective-permute-start | bytes 98312 | tf_op jit(solution)/shard_map/ppermute | solution.py:8
  267.4 5.0 %collective-permute-start.25 = (bf16[64,512]{1,0:T(8,128)(2,1)S(1)}, bf16[64,512]{1,0:T(8,128)(2,1)S(1)}, u32[]{:S(2)}, u32[]{:S(2)}) collective-permute-start(bf16[64,512]{1,0:T(8,128)(2,1)S(1)} %maximum_select_fusion.56), channel_id=1, source_target_pairs={{0,16},{8,24},{16,0},{24,8},{32,48},{40,56},{48,32},{56,40},{64,80... | collective-permute-start | bytes 196616 | tf_op jit(solution)/shard_map/ppermute | solution.py:8
  273.0 4.3 %collective-permute-start.26 = (bf16[64,256]{1,0:T(8,128)(2,1)S(1)}, bf16[64,256]{1,0:T(8,128)(2,1)S(1)}, u32[]{:S(2)}, u32[]{:S(2)}) collective-permute-start(bf16[64,256]{1,0:T(8,128)(2,1)S(1)} %get-tuple-element.12), channel_id=1, source_target_pairs={{0,8},{8,0},{16,24},{24,16},{32,40},{40,32},{48,56},{56,48},{64,72... | collective-permute-start | bytes 98312 | tf_op jit(solution)/shard_map/ppermute | solution.py:8
  277.3 5.0 %collective-permute-start.27 = (bf16[64,512]{1,0:T(8,128)(2,1)S(1)}, bf16[64,512]{1,0:T(8,128)(2,1)S(1)}, u32[]{:S(2)}, u32[]{:S(2)}) collective-permute-start(bf16[64,512]{1,0:T(8,128)(2,1)S(1)} %maximum_select_fusion.57), channel_id=1, source_target_pairs={{0,16},{8,24},{16,0},{24,8},{32,48},{40,56},{48,32},{56,40},{64,80... | collective-permute-start | bytes 196616 | tf_op jit(solution)/shard_map/ppermute | solution.py:8
  282.9 4.3 %collective-permute-start.28 = (bf16[64,256]{1,0:T(8,128)(2,1)S(1)}, bf16[64,256]{1,0:T(8,128)(2,1)S(1)}, u32[]{:S(2)}, u32[]{:S(2)}) collective-permute-start(bf16[64,256]{1,0:T(8,128)(2,1)S(1)} %get-tuple-element.9), channel_id=1, source_target_pairs={{0,8},{8,0},{16,24},{24,16},{32,40},{40,32},{48,56},{56,48},{64,72... | collective-permute-start | bytes 98312 | tf_op jit(solution)/shard_map/ppermute | solution.py:8
  287.1 5.0 %collective-permute-start.29 = (bf16[64,512]{1,0:T(8,128)(2,1)S(1)}, bf16[64,512]{1,0:T(8,128)(2,1)S(1)}, u32[]{:S(2)}, u32[]{:S(2)}) collective-permute-start(bf16[64,512]{1,0:T(8,128)(2,1)S(1)} %maximum_select_fusion.58), channel_id=1, source_target_pairs={{0,16},{8,24},{16,0},{24,8},{32,48},{40,56},{48,32},{56,40},{64,80... | collective-permute-start | bytes 196616 | tf_op jit(solution)/shard_map/ppermute | solution.py:8
  292.7 4.3 %collective-permute-start.30 = (bf16[64,256]{1,0:T(8,128)(2,1)S(1)}, bf16[64,256]{1,0:T(8,128)(2,1)S(1)}, u32[]{:S(2)}, u32[]{:S(2)}) collective-permute-start(bf16[64,256]{1,0:T(8,128)(2,1)S(1)} %get-tuple-element.6), channel_id=1, source_target_pairs={{0,8},{8,0},{16,24},{24,16},{32,40},{40,32},{48,56},{56,48},{64,72... | collective-permute-start | bytes 98312 | tf_op jit(solution)/shard_map/ppermute | solution.py:8
  297.0 5.0 %collective-permute-start.31 = (bf16[64,512]{1,0:T(8,128)(2,1)S(1)}, bf16[64,512]{1,0:T(8,128)(2,1)S(1)}, u32[]{:S(2)}, u32[]{:S(2)}) collective-permute-start(bf16[64,512]{1,0:T(8,128)(2,1)S(1)} %maximum_select_fusion.59), channel_id=1, source_target_pairs={{0,16},{8,24},{16,0},{24,8},{32,48},{40,56},{48,32},{56,40},{64,80... | collective-permute-start | bytes 196616 | tf_op jit(solution)/shard_map/ppermute | solution.py:8
  (13 other events, 119.5 us)
Sparse Core Ops, SparseCore 0:
  9.4 46.0 all-gather.8
  57.6 42.7 all-gather.10
  102.5 42.7 all-gather.12
  153.8 38.3 all-gather.14
where the time goes:
time: 311 us; the launch traced here: 310 us
  waiting for transfers between devices  124 us (40%)
  starting transfers between devices  99.7 us (32%)
  blocking collectives  23.5 us (8%)
  local copies, waits for them, and re-layouts  22.1 us (7%)
  matrix products  17.6 us (6%)
  between operations  13.9 us (4%)
  other arithmetic  9.2 us (3%)
    ppermute x32, starting transfers between devices, partner(): lax.ppermute(array, axis, [(i, i ^ 1 << distance) for i in range(lax.axis...  99.6 us
    ppermute x32, waiting for transfers between devices, partner(): lax.ppermute(array, axis, [(i, i ^ 1 << distance) for i in range(lax.axis...  73.6 us
    all_gather x2, waiting for transfers between devices, layer_rows(): lax.all_gather(recur_weights[layer], 'batch', axis=0, tiled=True)  39.8 us
    all_to_all x1, blocking collectives, local(): lax.all_to_all(outgoing, 'grp', split_axis=2, concat_axis=2, tiled=True)  23.5 us
    dot_general x16, matrix products, run_block(): jnp.dot(whole, w_rec, preferred_element_type=jnp.float32)  11.2 us
    all_gather x2, waiting for transfers between devices, layer_rows(): lax.all_gather(input_weights[layer], 'batch', axis=0, tiled=True)  10.4 us
    dot_general x2, matrix products, run_block(): jnp.dot(inputs.reshape(seqs * steps, width), w_in, preferred_element_type...  6.35 us
  transfers between devices with their start and end apart: 36, of which 32 were waited for; matrix products, arithmetic and copies ran while one was open for 13% of the time, Pallas kernels for 0%

commit v1 on v0

v1 whole, which is shorter than its diff:
```python
import jax
import jax.numpy as jnp
from jax import lax
from jax.experimental import pallas as pl
from jax.experimental.pallas import tpu as pltpu
from jax.sharding import PartitionSpec as P

MESH = pl.DeviceIdType.MESH
DEPTH = 4
SPLIT = 4
ITEMS = 14


def one_hot(rows, cols, target):
    row = lax.broadcasted_iota(jnp.int32, (rows, cols), 0)
    col = lax.broadcasted_iota(jnp.int32, (rows, cols), 1)
    return (col == target(row)).astype(jnp.float32).astype(jnp.bfloat16)


def sigmoid(x):
    return 0.5 * jnp.tanh(0.5 * x) + 0.5


def matmul(a, b):
    return jnp.dot(a, b, preferred_element_type=jnp.float32)


def kernel(
    tokens_hbm, win_ref, wrec_ref, bias_hbm, table_hbm, out_ref,
    tokens_ref, bias_ref, table_ref, w, wperm, x, proj, s0, s1, obuf, r, cell, pt, back,
    local_sem, wsend, wrecv, xsend, xrecv, ssend, srecv, osend, orecv, gsend, grecv,
):
    groups = lax.axis_size("grp") // SPLIT
    ring = lax.axis_size("batch")
    q = lax.axis_index("grp")
    z = lax.axis_index("batch")
    g = q // SPLIT
    m = q % SPLIT
    mates = (m + 1 - 2 * (m % 2), (m + 2) % SPLIT, SPLIT - 1 - m)

    here = m // 2 * 2
    there = 2 - here

    def mate(d):
        return (g * SPLIT + mates[d], z)

    up = (q, (z + 1) % ring)
    down = (q, (z + ring - 1) % ring)

    barrier = pltpu.get_barrier_semaphore()
    for device in (up, down, mate(0), mate(1), mate(2)):
        pl.semaphore_signal(barrier, inc=1, device_id=device, device_id_type=MESH)

    @pl.loop(1, groups)
    def _(d):
        other = (g + d) % groups
        pl.semaphore_signal(
            barrier, inc=1, device_id=(other * SPLIT + m, z), device_id_type=MESH
        )

    loads = []
    for layer in range(2):
        for kind, ref in enumerate((win_ref, wrec_ref)):
            arr = 2 * layer + kind
            load = pltpu.make_async_copy(
                ref.at[layer], w.at[arr, pl.ds(z * 8, 8)], local_sem.at[arr]
            )
            load.start()
            loads.append(load)

    small = []
    for n, (ref, copy) in enumerate(
        ((tokens_hbm, tokens_ref), (bias_hbm, bias_ref), (table_hbm, table_ref))
    ):
        load = pltpu.make_async_copy(ref, copy, local_sem.at[4 + n])
        load.start()
        small.append(load)

    def item(n, way, came):
        arr, j = n // ITEMS, n % ITEMS
        hop, piece = j // DEPTH, j % DEPTH
        if way == 0:
            origin = (z + 2 * ring - hop - came) % ring
            device = up
        else:
            piece = (piece + DEPTH // 2) % DEPTH
            origin = (z + hop + came) % ring
            device = down
        view = w.at[arr, pl.ds(origin * 8 + piece * 2, 2)]
        return pltpu.make_async_remote_copy(
            src_ref=view, dst_ref=view, send_sem=wsend.at[n, way], recv_sem=wrecv.at[n, way],
            device_id=device, device_id_type=MESH,
        )

    def tick(n, more=True):
        for way in range(2):
            item(n, way, 1).wait_recv()
            if more:
                item(n + DEPTH, way, 0).start()
            item(n, way, 0).wait_send()

    def state_copy(states, layer, t, h, d, owner):
        view = states.at[t, h, owner]
        return pltpu.make_async_remote_copy(
            src_ref=view, dst_ref=view,
            send_sem=ssend.at[layer, t, h, d], recv_sem=srecv.at[layer, t, h, d],
            device_id=mate(d), device_id_type=MESH,
        )

    def input_copy(d, owner):
        view = x.at[owner]
        return pltpu.make_async_remote_copy(
            src_ref=view, dst_ref=view, send_sem=xsend.at[d], recv_sem=xrecv.at[d],
            device_id=mate(d), device_id_type=MESH,
        )

    def mixed_copy(p, d, owner):
        view = r.at[p, owner]
        return pltpu.make_async_remote_copy(
            src_ref=view, dst_ref=view, send_sem=gsend.at[p, d], recv_sem=grecv.at[p, d],
            device_id=mate(d), device_id_type=MESH,
        )

    def shuffled_all(p):
        return pltpu.make_async_remote_copy(
            src_ref=obuf.at[p, pl.ds(0, groups - 1)], dst_ref=r.at[p, m, pl.ds(0, groups - 1)],
            send_sem=osend.at[p], recv_sem=orecv.at[p], device_id=mate(0), device_id_type=MESH,
        )

    for load in loads:
        load.wait()
    pl.semaphore_wait(barrier, 5 + groups - 1)
    for n in range(DEPTH):
        for way in range(2):
            item(n, way, 0).start()

    for load in small:
        load.wait()

    rows = tokens_ref.shape[0]
    steps = proj.shape[0]
    seqs = rows // steps
    half = seqs // 2
    order = one_hot(rows, rows, lambda a: (a & (seqs - 1)) * steps + (a >> seqs.bit_length() - 1))
    x[m] = matmul(order, tokens_ref[...]).astype(jnp.bfloat16)
    for d in (2, 1, 0):
        input_copy(d, m).start()
    back[...] = one_hot(rows, rows, lambda a: (a & (steps - 1)) * seqs + (a >> steps.bit_length() - 1))

    lanes = 128
    per_row = lanes // 4
    odd = q // per_row
    row = lax.broadcasted_iota(jnp.int32, (lanes, lanes), 0)
    col = lax.broadcasted_iota(jnp.int32, (lanes, lanes), 1)
    mine = ((col >> 2) == q % per_row) & ((row & 1) == odd)
    entries = jnp.where(mine, table_ref[...] - q * 256, 0).astype(jnp.float32).astype(jnp.bfloat16)
    spread = matmul(one_hot(256, lanes, lambda a: (a >> 2) * 2 + odd), entries)
    row = lax.broadcasted_iota(jnp.int32, (256, lanes), 0)
    col = lax.broadcasted_iota(jnp.int32, (256, lanes), 1)
    wanted = col == (q % per_row) * 4 + (row & 3)
    picked = jnp.sum(jnp.where(wanted, spread, 0.0), axis=1, keepdims=True)
    channel = lax.broadcasted_iota(jnp.int32, (256, 256), 1).astype(jnp.float32)
    pt[...] = jnp.where(channel == picked, 1.0, 0.0).astype(jnp.bfloat16)

    def rows_of(arr, i):
        return w.at[arr, pl.ds(i * 16, 16)]

    @pl.loop(0, ITEMS)
    def _(n):
        tick(n)

    for d in range(3):
        input_copy(d, mates[d]).wait_recv()
        input_copy(d, m).wait_send()

    @pl.loop(0, 4)
    def _(c):
        cols = pl.ds(pl.multiple_of(c * 256, 256), 256)
        total = bias_ref[0:1, cols]
        for i in range(SPLIT):
            total = total + matmul(x[i], w[0, pl.ds(i * 16, 16), :, cols].reshape(256, 256))
        proj[:, :, :, cols] = total.reshape(steps, 2, half, 256)
        tick(ITEMS + c)

    def update(gate, states, layer, t, h, first=False):
        ingate = sigmoid(gate(0))
        cellgate = jnp.tanh(gate(2))
        now = ingate * cellgate
        if not first:
            now = now + sigmoid(gate(1)) * cell[h]
        outgate = sigmoid(gate(3))
        cell[h] = now
        states[t, h, m] = (outgate * jnp.tanh(now)).astype(jnp.bfloat16)

    def send_state(states, layer, t, h):
        for d in (1, 2, 0):
            state_copy(states, layer, t, h, d, m).start()

    def start(states, layer):
        for h in range(2):
            update(lambda k: proj[0, h, :, k * 256 : k * 256 + 256], states, layer, 0, h, first=True)
            send_state(states, layer, 0, h)

    def step(states, layer, t, h):
        arr = 2 * layer + 1

        def pair(first):
            both = [states[t - 1, h, first + i] for i in range(2)]
            return jnp.concatenate(both, axis=1)

        def product(lhs, first, k):
            cols = slice(k * 256, k * 256 + 256)
            return matmul(lhs, w[arr, pl.ds(first * 16, 32), :, cols].reshape(512, 256))

        state_copy(states, layer, t - 1, h, 0, mates[0]).wait_recv()
        lhs = pair(here)
        near = [
            proj[t, h, :, k * 256 : k * 256 + 256] + product(lhs, here, k) for k in range(4)
        ]
        for d in (1, 2):
            state_copy(states, layer, t - 1, h, d, mates[d]).wait_recv()
        lhs = pair(there)
        update(lambda k: near[k] + product(lhs, there, k), states, layer, t, h)

        @pl.when(t < steps - 1)
        def _():
            send_state(states, layer, t, h)

        for d in range(3):
            state_copy(states, layer, t - 1, h, d, m).wait_send()

    def forward(p):
        shuffled_all(p).wait_recv()
        for d in range(3):
            mixed_copy(p, d, m).start()

    start(s0, 0)

    @pl.loop(ITEMS + 4, 2 * ITEMS)
    def _(n):
        tick(n)

    @pl.loop(1, steps)
    def _(t):
        p = t // 2
        n = 2 * ITEMS + 3 * (t - 1)
        step(s0, 0, t, 0)
        tick(n)
        step(s0, 0, t, 1)
        tick(n + 1)

        @pl.when(t % 2 == 1)
        def _():
            pair = jnp.concatenate([s0[t - 1 + h // 2, h % 2, m] for h in range(4)], axis=0)
            moved = lax.dot_general(
                pt[...], pair, (((1,), (1,)), ((), ())), preferred_element_type=jnp.float32
            )
            obuf[p] = moved.astype(jnp.bfloat16).reshape(groups, 16, 128)
            r[p, m, g] = obuf[p, g]

            @pl.loop(1, groups)
            def _(d):
                other = (g + d) % groups
                pltpu.make_async_remote_copy(
                    src_ref=obuf.at[p, other], dst_ref=r.at[p, m, g],
                    send_sem=osend.at[p], recv_sem=orecv.at[p],
                    device_id=(other * SPLIT + m, z), device_id_type=MESH,
                ).start()

        @pl.when(t % 2 == 0)
        def _():
            forward(p - 1)

        tick(n + 2)

    swap = one_hot(64, 64, lambda a: ((a >> 2) & 3) * 16 + (a >> 4) * 4 + (a & 3))

    @pl.loop(0, groups)
    def _(i):
        block = jnp.concatenate([w[2, j * 16 + i] for j in range(SPLIT)], axis=0)
        block = matmul(swap, block).astype(jnp.bfloat16).reshape(SPLIT, 16, 1024)
        for j in range(SPLIT):
            wperm[j * 16 + i] = block[j]

        @pl.when(i % 8 == 7)
        def _():
            tick(4 * ITEMS - 7 + i // 8)

    tick(4 * ITEMS - 5)
    forward(steps // 2 - 1)

    @pl.loop(0, steps // 2)
    def _(p):
        shuffled_all(p).wait_send()
        for d in range(3):
            mixed_copy(p, d, mates[d]).wait_recv()
            mixed_copy(p, d, m).wait_send()
        total = lax.dot_general(
            r[p].reshape(1024, 128), wperm[...].reshape(1024, 1024),
            (((0,), (0,)), ((), ())), preferred_element_type=jnp.float32,
        )
        proj[pl.ds(2 * p, 2)] = (total + bias_ref[1:2, :]).reshape(2, 2, half, 1024)

    start(s1, 1)

    for n in range(4 * ITEMS - DEPTH, 4 * ITEMS):
        tick(n, False)

    @pl.loop(1, steps)
    def _(t):
        for h in range(2):
            step(s1, 1, t, h)

    states = jnp.concatenate([s1[h // 2, h % 2, m] for h in range(2 * steps)], axis=0)
    out_ref[...] = matmul(back[...], states).astype(jnp.bfloat16)


def local(tokens, input_weights, recur_weights, biases, shuffle):
    seqs, steps, units = tokens.shape
    depth = input_weights.shape[1]
    bf16 = jnp.bfloat16
    vmem = pl.BlockSpec(memory_space=pltpu.VMEM)
    hbm = pl.BlockSpec(memory_space=pl.ANY)
    dma = pltpu.SemaphoreType.DMA
    pairs = steps // 2
    out = pl.pallas_call(
        kernel,
        out_shape=jax.ShapeDtypeStruct((seqs * steps, units), bf16),
        in_specs=[hbm] * 5,
        out_specs=vmem,
        scratch_shapes=[
            pltpu.VMEM((seqs * steps, units), bf16),
            pltpu.VMEM((2, 1024), jnp.float32),
            pltpu.VMEM((128, 128), jnp.int32),
            pltpu.VMEM((4, 64, 16, 1024), bf16),
            pltpu.VMEM((64, 16, 1024), bf16),
            pltpu.VMEM((SPLIT, seqs * steps, units), bf16),
            pltpu.VMEM((steps, 2, seqs // 2, 1024), jnp.float32),
            pltpu.VMEM((steps, 2, SPLIT, seqs // 2, units), bf16),
            pltpu.VMEM((steps, 2, SPLIT, seqs // 2, units), bf16),
            pltpu.VMEM((pairs, 16, 16, 128), bf16),
            pltpu.VMEM((pairs, SPLIT, 16, 16, 128), bf16),
            pltpu.VMEM((2, seqs // 2, units), jnp.float32),
            pltpu.VMEM((256, 256), bf16),
            pltpu.VMEM((512, 512), bf16),
            dma((7,)),
            dma((4 * ITEMS, 2)),
            dma((4 * ITEMS, 2)),
            dma((3,)),
            dma((3,)),
            dma((2, steps, 2, 3)),
            dma((2, steps, 2, 3)),
            dma((pairs,)),
            dma((pairs,)),
            dma((pairs, 3)),
            dma((pairs, 3)),
        ],
        compiler_params=pltpu.CompilerParams(
            collective_id=0, has_side_effects=True, vmem_limit_bytes=63 * 1024 * 1024
        ),
    )(
        tokens.reshape(seqs * steps, units),
        input_weights.reshape(2, depth // 16, 16, 1024),
        recur_weights.reshape(2, depth // 16, 16, 1024),
        biases,
        shuffle.reshape(128, 128),
    )
    return out.reshape(seqs, steps, units)


def solution(mesh):
    return jax.shard_map(
        local,
        mesh=mesh,
        in_specs=(
            P("batch", None, "grp"),
            P(None, "batch", "grp"),
            P(None, "batch", "grp"),
            P(None, "grp"),
            P(),
        ),
        out_specs=P("batch", None, "grp"),
        check_vma=False,
    )
```

time: 311 us -> 128 us (0.41)
  Pallas kernels: 0 us -> 126 us
  waiting for transfers between devices: 124 us -> 0 us
  starting transfers between devices: 99.7 us -> 0 us
  blocking collectives: 23.5 us -> 0 us
  local copies, waits for them, and re-layouts: 22.1 us -> 1.67 us
  matrix products: 17.6 us -> 0 us
  between operations: 13.9 us -> 0.01 us
  other arithmetic: 9.2 us -> 0 us
    pallas_call x0 -> x1, Pallas kernels: none -> 126 us  [local(): pl.pallas_call(kernel, out_shape=jax.ShapeDtypeStruct((seqs * steps, unit...]
    ppermute x32 -> x0, starting transfers between devices: 99.6 us -> none  [partner(): lax.ppermute(array, axis, [(i, i ^ 1 << distance) for i in range(lax.axis...]
    ppermute x32 -> x0, waiting for transfers between devices: 73.6 us -> none  [partner(): lax.ppermute(array, axis, [(i, i ^ 1 << distance) for i in range(lax.axis...]
    all_gather x4 -> x0, waiting for transfers between devices: 50.3 us -> none  [the longest x2 39.8 us: layer_rows(): lax.all_gather(recur_weights[layer], 'batch', axis=0, tiled=True)]
    all_to_all x1 -> x0, blocking collectives: 23.5 us -> none  [local(): lax.all_to_all(outgoing, 'grp', split_axis=2, concat_axis=2, tiled=True)]
    dot_general x18 -> x0, matrix products: 17.6 us -> none  [the longest x16 11.2 us: run_block(): jnp.dot(whole, w_rec, preferred_element_type=jnp.float32)]
    slice x4 -> x0, local copies, waits for them, and re-layouts: 6.03 us -> none  [the longest x1 2.18 us: run_block(): proj[:, step] + jnp.dot(whole, w_rec, preferred_element_type=jnp.float32)]
    select_n x19 -> x0, other arithmetic: 5.78 us -> none  [the longest x18 5.78 us: order_pair(): jnp.where(lower, jnp.concatenate([mine, other], axis=-1), jnp.concatenate...]
  transfers between devices with their start and end apart: 36 -> 0, of which waited for: 32 -> 0; matrix products, arithmetic and copies ran while one was open for 13% -> 0% of each run, Pallas kernels for 0% -> 0%
where the time goes in v1:
time: 128 us
  Pallas kernels  126 us (98%)
  local copies, waits for them, and re-layouts  1.67 us (1%)
    pallas_call x1, Pallas kernels, local(): pl.pallas_call(kernel, out_shape=jax.ShapeDtypeStruct((seqs * steps, unit...  126 us

profile of v1, /device:TPU:1, one launch (start us, length us, event | category | flops | bytes accessed | tf_op | source)
XLA Modules:
  0.0 128.0 jit_solution(15743288270454177628)
XLA Ops:
  0.0 126.3 %shard_map.55 = bf16[512,256]{1,0:T(8,128)(2,1)} custom-call(bf16[512,256]{1,0:T(8,128)(2,1)} %bitcast.8, bf16[2,8,16,1024]{3,2,1,0:T(8,128)(2,1)} %bitcast.6, bf16[2,8,16,1024]{3,2,1,0:T(8,128)(2,1)} %bitcast.7, f32[2,1024]{1,0:T(2,128)} %bias_hbm.1, s32[128,128]{1,0:T(8,128)} %bitcast.9), custom_call_target="tpu_custom_call" | custom-call | tf_op jit(solution)/shard_map/pallas_call | solution.py:326
  126.3 1.7 %copy.7 = bf16[64,8,256]{2,1,0:T(8,128)(2,1)} copy(bf16[64,8,256]{2,1,0:T(8,128)(2,1)} %bitcast.5) | data formatting | bytes 524288

commit v2 on v1

--- a/solution.py
+++ b/solution.py
@@ -208,19 +208,15 @@
             both = [states[t - 1, h, first + i] for i in range(2)]
             return jnp.concatenate(both, axis=1)
 
-        def product(lhs, first, k):
-            cols = slice(k * 256, k * 256 + 256)
-            return matmul(lhs, w[arr, pl.ds(first * 16, 32), :, cols].reshape(512, 256))
+        def product(first):
+            return matmul(pair(first), w[arr, pl.ds(first * 16, 32)].reshape(512, 1024))
 
         state_copy(states, layer, t - 1, h, 0, mates[0]).wait_recv()
-        lhs = pair(here)
-        near = [
-            proj[t, h, :, k * 256 : k * 256 + 256] + product(lhs, here, k) for k in range(4)
-        ]
+        pre = proj[t, h] + product(here)
         for d in (1, 2):
             state_copy(states, layer, t - 1, h, d, mates[d]).wait_recv()
-        lhs = pair(there)
-        update(lambda k: near[k] + product(lhs, there, k), states, layer, t, h)
+        pre = pre + product(there)
+        update(lambda k: pre[:, k * 256 : k * 256 + 256], states, layer, t, h)
 
         @pl.when(t < steps - 1)
         def _():

time: 128 us -> 128 us (level)
  no operation moved by 1% of the time
where the time goes in v2:
time: 128 us
  Pallas kernels  126 us (98%)
  local copies, waits for them, and re-layouts  1.67 us (1%)
    pallas_call x1, Pallas kernels, local(): pl.pallas_call(kernel, out_shape=jax.ShapeDtypeStruct((seqs * steps, unit...  126 us

profile of v2, /device:TPU:1, one launch (start us, length us, event | category | flops | bytes accessed | tf_op | source)
XLA Modules:
  0.0 127.9 jit_solution(3174726641299663814)
XLA Ops:
  0.0 126.3 %shard_map.55 = bf16[512,256]{1,0:T(8,128)(2,1)} custom-call(bf16[512,256]{1,0:T(8,128)(2,1)} %bitcast.8, bf16[2,8,16,1024]{3,2,1,0:T(8,128)(2,1)} %bitcast.6, bf16[2,8,16,1024]{3,2,1,0:T(8,128)(2,1)} %bitcast.7, f32[2,1024]{1,0:T(2,128)} %bias_hbm.1, s32[128,128]{1,0:T(8,128)} %bitcast.9), custom_call_target="tpu_custom_call" | custom-call | tf_op jit(solution)/shard_map/pallas_call | solution.py:322
  126.3 1.7 %copy.7 = bf16[64,8,256]{2,1,0:T(8,128)(2,1)} copy(bf16[64,8,256]{2,1,0:T(8,128)(2,1)} %bitcast.5) | data formatting | bytes 524288

commit v3 on v2

--- a/solution.py
+++ b/solution.py
@@ -8,6 +8,7 @@
 MESH = pl.DeviceIdType.MESH
 DEPTH = 4
 SPLIT = 4
+PARTS = 1
 ITEMS = 14
 
 
@@ -140,7 +141,7 @@
     rows = tokens_ref.shape[0]
     steps = proj.shape[0]
     seqs = rows // steps
-    half = seqs // 2
+    part = seqs // PARTS
     order = one_hot(rows, rows, lambda a: (a & (seqs - 1)) * steps + (a >> seqs.bit_length() - 1))
     x[m] = matmul(order, tokens_ref[...]).astype(jnp.bfloat16)
     for d in (2, 1, 0):
@@ -179,7 +180,7 @@
         total = bias_ref[0:1, cols]
         for i in range(SPLIT):
             total = total + matmul(x[i], w[0, pl.ds(i * 16, 16), :, cols].reshape(256, 256))
-        proj[:, :, :, cols] = total.reshape(steps, 2, half, 256)
+        proj[:, :, :, cols] = total.reshape(steps, PARTS, part, 256)
         tick(ITEMS + c)
 
     def update(gate, states, layer, t, h, first=False):
@@ -197,7 +198,7 @@
             state_copy(states, layer, t, h, d, m).start()
 
     def start(states, layer):
-        for h in range(2):
+        for h in range(PARTS):
             update(lambda k: proj[0, h, :, k * 256 : k * 256 + 256], states, layer, 0, h, first=True)
             send_state(states, layer, 0, h)
 
@@ -242,12 +243,13 @@
         n = 2 * ITEMS + 3 * (t - 1)
         step(s0, 0, t, 0)
         tick(n)
-        step(s0, 0, t, 1)
+        for h in range(1, PARTS):
+            step(s0, 0, t, h)
         tick(n + 1)
 
         @pl.when(t % 2 == 1)
         def _():
-            pair = jnp.concatenate([s0[t - 1 + h // 2, h % 2, m] for h in range(4)], axis=0)
+            pair = jnp.concatenate([s0[t - 1 + h // PARTS, h % PARTS, m] for h in range(2 * PARTS)], axis=0)
             moved = lax.dot_general(
                 pt[...], pair, (((1,), (1,)), ((), ())), preferred_element_type=jnp.float32
             )
@@ -285,8 +287,7 @@
     tick(4 * ITEMS - 5)
     forward(steps // 2 - 1)
 
-    @pl.loop(0, steps // 2)
-    def _(p):
+    def project_mixed(p):
         shuffled_all(p).wait_send()
         for d in range(3):
             mixed_copy(p, d, mates[d]).wait_recv()
@@ -295,7 +296,11 @@
             r[p].reshape(1024, 128), wperm[...].reshape(1024, 1024),
             (((0,), (0,)), ((), ())), preferred_element_type=jnp.float32,
         )
-        proj[pl.ds(2 * p, 2)] = (total + bias_ref[1:2, :]).reshape(2, 2, half, 1024)
+        proj[pl.ds(2 * p, 2)] = (total + bias_ref[1:2, :]).reshape(2, PARTS, part, 1024)
+
+    @pl.loop(0, steps // 2 - 1)
+    def _(p):
+        project_mixed(p)
 
     start(s1, 1)
 
@@ -304,10 +309,14 @@
 
     @pl.loop(1, steps)
     def _(t):
-        for h in range(2):
+        for h in range(PARTS):
             step(s1, 1, t, h)
 
-    states = jnp.concatenate([s1[h // 2, h % 2, m] for h in range(2 * steps)], axis=0)
+        @pl.when(t == 1)
+        def _():
+            project_mixed(steps // 2 - 1)
+
+    states = jnp.concatenate([s1[h // PARTS, h % PARTS, m] for h in range(PARTS * steps)], axis=0)
     out_ref[...] = matmul(back[...], states).astype(jnp.bfloat16)
 
 
@@ -331,12 +340,12 @@
             pltpu.VMEM((4, 64, 16, 1024), bf16),
             pltpu.VMEM((64, 16, 1024), bf16),
             pltpu.VMEM((SPLIT, seqs * steps, units), bf16),
-            pltpu.VMEM((steps, 2, seqs // 2, 1024), jnp.float32),
-            pltpu.VMEM((steps, 2, SPLIT, seqs // 2, units), bf16),
-            pltpu.VMEM((steps, 2, SPLIT, seqs // 2, units), bf16),
+            pltpu.VMEM((steps, PARTS, seqs // PARTS, 1024), jnp.float32),
+            pltpu.VMEM((steps, PARTS, SPLIT, seqs // PARTS, units), bf16),
+            pltpu.VMEM((steps, PARTS, SPLIT, seqs // PARTS, units), bf16),
             pltpu.VMEM((pairs, 16, 16, 128), bf16),
             pltpu.VMEM((pairs, SPLIT, 16, 16, 128), bf16),
-            pltpu.VMEM((2, seqs // 2, units), jnp.float32),
+            pltpu.VMEM((PARTS, seqs // PARTS, units), jnp.float32),
             pltpu.VMEM((256, 256), bf16),
             pltpu.VMEM((512, 512), bf16),
             dma((7,)),
@@ -344,8 +353,8 @@
             dma((4 * ITEMS, 2)),
             dma((3,)),
             dma((3,)),
-            dma((2, steps, 2, 3)),
-            dma((2, steps, 2, 3)),
+            dma((2, steps, PARTS, 3)),
+            dma((2, steps, PARTS, 3)),
             dma((pairs,)),
             dma((pairs,)),
             dma((pairs, 3)),

time: 128 us -> 127 us (level)
    pallas_call x1, Pallas kernels: 126 us -> 125 us  [local(): pl.pallas_call(kernel, out_shape=jax.ShapeDtypeStruct((seqs * steps, unit...]
where the time goes in v3:
time: 127 us; the launch traced here: 126 us
  Pallas kernels  125 us (98%)
  local copies, waits for them, and re-layouts  1.67 us (1%)
    pallas_call x1, Pallas kernels, local(): pl.pallas_call(kernel, out_shape=jax.ShapeDtypeStruct((seqs * steps, unit...  125 us

profile of v3, /device:TPU:1, one launch (start us, length us, event | category | flops | bytes accessed | tf_op | source)
XLA Modules:
  0.0 126.5 jit_solution(9244437213619619999)
XLA Ops:
  0.0 124.8 %shard_map.55 = bf16[512,256]{1,0:T(8,128)(2,1)} custom-call(bf16[512,256]{1,0:T(8,128)(2,1)} %bitcast.8, bf16[2,8,16,1024]{3,2,1,0:T(8,128)(2,1)} %bitcast.6, bf16[2,8,16,1024]{3,2,1,0:T(8,128)(2,1)} %bitcast.7, f32[2,1024]{1,0:T(2,128)} %bias_hbm.1, s32[128,128]{1,0:T(8,128)} %bitcast.9), custom_call_target="tpu_custom_call" | custom-call | tf_op jit(solution)/shard_map/pallas_call | solution.py:331
  124.8 1.7 %copy.7 = bf16[64,8,256]{2,1,0:T(8,128)(2,1)} copy(bf16[64,8,256]{2,1,0:T(8,128)(2,1)} %bitcast.5) | data formatting | bytes 524288

commit v4 on v3

--- a/solution.py
+++ b/solution.py
@@ -28,8 +28,8 @@
 
 def kernel(
     tokens_hbm, win_ref, wrec_ref, bias_hbm, table_hbm, out_ref,
-    tokens_ref, bias_ref, table_ref, w, wperm, x, proj, s0, s1, obuf, r, cell, pt, back,
-    local_sem, wsend, wrecv, xsend, xrecv, ssend, srecv, osend, orecv, gsend, grecv,
+    tokens_ref, bias_ref, table_ref, w, wperm, x, proj, s0, s1, obuf, r, cell, pt,
+    local_sem, wsend, wrecv, xsend, xrecv, ssend, srecv, osend, orecv, gsend, grecv, done,
 ):
     groups = lax.axis_size("grp") // SPLIT
     ring = lax.axis_size("batch")
@@ -40,24 +40,12 @@
     mates = (m + 1 - 2 * (m % 2), (m + 2) % SPLIT, SPLIT - 1 - m)
 
     here = m // 2 * 2
-    there = 2 - here
 
     def mate(d):
         return (g * SPLIT + mates[d], z)
 
     up = (q, (z + 1) % ring)
     down = (q, (z + ring - 1) % ring)
-
-    barrier = pltpu.get_barrier_semaphore()
-    for device in (up, down, mate(0), mate(1), mate(2)):
-        pl.semaphore_signal(barrier, inc=1, device_id=device, device_id_type=MESH)
-
-    @pl.loop(1, groups)
-    def _(d):
-        other = (g + d) % groups
-        pl.semaphore_signal(
-            barrier, inc=1, device_id=(other * SPLIT + m, z), device_id_type=MESH
-        )
 
     loads = []
     for layer in range(2):
@@ -76,6 +64,17 @@
         load = pltpu.make_async_copy(ref, copy, local_sem.at[4 + n])
         load.start()
         small.append(load)
+
+    barrier = pltpu.get_barrier_semaphore()
+    for device in (up, down, mate(0), mate(1), mate(2)):
+        pl.semaphore_signal(barrier, inc=1, device_id=device, device_id_type=MESH)
+
+    @pl.loop(1, groups)
+    def _(d):
+        other = (g + d) % groups
+        pl.semaphore_signal(
+            barrier, inc=1, device_id=(other * SPLIT + m, z), device_id_type=MESH
+        )
 
     def item(n, way, came):
         arr, j = n // ITEMS, n % ITEMS
@@ -128,14 +127,13 @@
             send_sem=osend.at[p], recv_sem=orecv.at[p], device_id=mate(0), device_id_type=MESH,
         )
 
-    for load in loads:
-        load.wait()
+    loads[0].wait()
     pl.semaphore_wait(barrier, 5 + groups - 1)
     for n in range(DEPTH):
         for way in range(2):
             item(n, way, 0).start()
 
-    for load in small:
+    for load in small + loads[1:]:
         load.wait()
 
     rows = tokens_ref.shape[0]
@@ -146,7 +144,6 @@
     x[m] = matmul(order, tokens_ref[...]).astype(jnp.bfloat16)
     for d in (2, 1, 0):
         input_copy(d, m).start()
-    back[...] = one_hot(rows, rows, lambda a: (a & (steps - 1)) * seqs + (a >> steps.bit_length() - 1))
 
     lanes = 128
     per_row = lanes // 4
@@ -205,18 +202,13 @@
     def step(states, layer, t, h):
         arr = 2 * layer + 1
 
-        def pair(first):
-            both = [states[t - 1, h, first + i] for i in range(2)]
-            return jnp.concatenate(both, axis=1)
-
-        def product(first):
-            return matmul(pair(first), w[arr, pl.ds(first * 16, 32)].reshape(512, 1024))
-
         state_copy(states, layer, t - 1, h, 0, mates[0]).wait_recv()
-        pre = proj[t, h] + product(here)
+        near = jnp.concatenate([states[t - 1, h, here + i] for i in range(2)], axis=1)
+        pre = proj[t, h] + matmul(near, w[arr, pl.ds(here * 16, 32)].reshape(512, 1024))
         for d in (1, 2):
             state_copy(states, layer, t - 1, h, d, mates[d]).wait_recv()
-        pre = pre + product(there)
+            far = states[t - 1, h, mates[d]]
+            pre = pre + matmul(far, w[arr, pl.ds(mates[d] * 16, 16)].reshape(256, 1024))
         update(lambda k: pre[:, k * 256 : k * 256 + 256], states, layer, t, h)
 
         @pl.when(t < steps - 1)
@@ -302,6 +294,12 @@
     def _(p):
         project_mixed(p)
 
+    def stored(t):
+        return pltpu.make_async_copy(s1.at[t, 0, m], out_ref.at[t], done.at[t])
+
+    def store(t):
+        stored(t).start()
+
     start(s1, 1)
 
     for n in range(4 * ITEMS - DEPTH, 4 * ITEMS):
@@ -311,28 +309,31 @@
     def _(t):
         for h in range(PARTS):
             step(s1, 1, t, h)
+        store(t - 1)
 
         @pl.when(t == 1)
         def _():
             project_mixed(steps // 2 - 1)
 
-    states = jnp.concatenate([s1[h // PARTS, h % PARTS, m] for h in range(PARTS * steps)], axis=0)
-    out_ref[...] = matmul(back[...], states).astype(jnp.bfloat16)
+    store(steps - 1)
+
+    @pl.loop(0, steps)
+    def _(t):
+        stored(t).wait()
 
 
 def local(tokens, input_weights, recur_weights, biases, shuffle):
     seqs, steps, units = tokens.shape
     depth = input_weights.shape[1]
     bf16 = jnp.bfloat16
-    vmem = pl.BlockSpec(memory_space=pltpu.VMEM)
     hbm = pl.BlockSpec(memory_space=pl.ANY)
     dma = pltpu.SemaphoreType.DMA
     pairs = steps // 2
     out = pl.pallas_call(
         kernel,
-        out_shape=jax.ShapeDtypeStruct((seqs * steps, units), bf16),
+        out_shape=jax.ShapeDtypeStruct((steps, seqs, units), bf16),
         in_specs=[hbm] * 5,
-        out_specs=vmem,
+        out_specs=hbm,
         scratch_shapes=[
             pltpu.VMEM((seqs * steps, units), bf16),
             pltpu.VMEM((2, 1024), jnp.float32),
@@ -347,7 +348,6 @@
             pltpu.VMEM((pairs, SPLIT, 16, 16, 128), bf16),
             pltpu.VMEM((PARTS, seqs // PARTS, units), jnp.float32),
             pltpu.VMEM((256, 256), bf16),
-            pltpu.VMEM((512, 512), bf16),
             dma((7,)),
             dma((4 * ITEMS, 2)),
             dma((4 * ITEMS, 2)),
@@ -359,6 +359,7 @@
             dma((pairs,)),
             dma((pairs, 3)),
             dma((pairs, 3)),
+            dma((steps,)),
         ],
         compiler_params=pltpu.CompilerParams(
             collective_id=0, has_side_effects=True, vmem_limit_bytes=63 * 1024 * 1024
@@ -370,7 +371,7 @@
         biases,
         shuffle.reshape(128, 128),
     )
-    return out.reshape(seqs, steps, units)
+    return jnp.transpose(out, (1, 0, 2))
 
 
 def solution(mesh):

time: 127 us -> 126 us (level)
    transpose x0 -> x1, local copies, waits for them, and re-layouts: none -> 1.8 us  [local(): return jnp.transpose(out, (1, 0, 2))]
    unnamed x1 -> x0, local copies, waits for them, and re-layouts: 1.67 us -> none
where the time goes in v4:
time: 126 us
  Pallas kernels  124 us (98%)
  local copies, waits for them, and re-layouts  1.8 us (1%)
    pallas_call x1, Pallas kernels, local(): pl.pallas_call(kernel, out_shape=jax.ShapeDtypeStruct((steps, seqs, units...  124 us

profile of v4, /device:TPU:1, one launch (start us, length us, event | category | flops | bytes accessed | tf_op | source)
XLA Modules:
  0.0 126.0 jit_solution(7963054125168817314)
XLA Ops:
  0.0 124.2 %shard_map.55 = bf16[8,64,256]{2,1,0:T(8,128)(2,1)} custom-call(bf16[512,256]{1,0:T(8,128)(2,1)} %bitcast.8, bf16[2,8,16,1024]{3,2,1,0:T(8,128)(2,1)} %bitcast.6, bf16[2,8,16,1024]{3,2,1,0:T(8,128)(2,1)} %bitcast.7, f32[2,1024]{1,0:T(2,128)} %bias_hbm.1, s32[128,128]{1,0:T(8,128)} %bitcast.9), custom_call_target="tpu_custom_call" | custom-call | tf_op jit(solution)/shard_map/pallas_call | solution.py:332
  124.2 1.8 %copy.6 = bf16[64,8,256]{2,1,0:T(8,128)(2,1)} copy(bf16[64,8,256]{2,0,1:T(8,128)(2,1)} %bitcast.5) | data formatting | bytes 524288 | tf_op jit(solution)/shard_map/transpose | solution.py:374

commit v5 on v4

--- a/solution.py
+++ b/solution.py
@@ -263,21 +263,25 @@
 
         tick(n + 2)
 
-    swap = one_hot(64, 64, lambda a: ((a >> 2) & 3) * 16 + (a >> 4) * 4 + (a & 3))
-
-    @pl.loop(0, groups)
-    def _(i):
-        block = jnp.concatenate([w[2, j * 16 + i] for j in range(SPLIT)], axis=0)
-        block = matmul(swap, block).astype(jnp.bfloat16).reshape(SPLIT, 16, 1024)
-        for j in range(SPLIT):
-            wperm[j * 16 + i] = block[j]
-
-        @pl.when(i % 8 == 7)
-        def _():
-            tick(4 * ITEMS - 7 + i // 8)
+    swap = one_hot(
+        256, 256, lambda a: (a & 192) + ((a >> 2) & 3) * 16 + ((a >> 4) & 3) * 4 + (a & 3)
+    )
+
+    @pl.loop(0, groups // 4)
+    def _(v):
+        block = jnp.concatenate(
+            [w[2, j * 16 + 4 * v + i] for i in range(4) for j in range(SPLIT)], axis=0
+        )
+        block = matmul(swap, block).astype(jnp.bfloat16).reshape(4, SPLIT, 16, 1024)
+        for i in range(4):
+            for j in range(SPLIT):
+                wperm[j * 16 + 4 * v + i] = block[i, j]
+
+        @pl.when(v % 2 == 1)
+        def _():
+            tick(4 * ITEMS - 7 + v // 2)
 
     tick(4 * ITEMS - 5)
-    forward(steps // 2 - 1)
 
     def project_mixed(p):
         shuffled_all(p).wait_send()
@@ -290,17 +294,20 @@
         )
         proj[pl.ds(2 * p, 2)] = (total + bias_ref[1:2, :]).reshape(2, PARTS, part, 1024)
 
-    @pl.loop(0, steps // 2 - 1)
+    project_mixed(0)
+
+    def stored(t):
+        return pltpu.make_async_copy(s1.at[t, 0, m], out_ref.at[t], done.at[t])
+
+    def store(t):
+        stored(t).start()
+
+    start(s1, 1)
+    forward(steps // 2 - 1)
+
+    @pl.loop(1, steps // 2 - 1)
     def _(p):
         project_mixed(p)
-
-    def stored(t):
-        return pltpu.make_async_copy(s1.at[t, 0, m], out_ref.at[t], done.at[t])
-
-    def store(t):
-        stored(t).start()
-
-    start(s1, 1)
 
     for n in range(4 * ITEMS - DEPTH, 4 * ITEMS):
         tick(n, False)

time: 126 us -> 125 us (level)
    pallas_call x1, Pallas kernels: 124 us -> 123 us  [local(): pl.pallas_call(kernel, out_shape=jax.ShapeDtypeStruct((steps, seqs, units...]
where the time goes in v5:
time: 125 us
  Pallas kernels  123 us (98%)
  local copies, waits for them, and re-layouts  1.8 us (1%)
    pallas_call x1, Pallas kernels, local(): pl.pallas_call(kernel, out_shape=jax.ShapeDtypeStruct((steps, seqs, units...  123 us

profile of v5, /device:TPU:1, one launch (start us, length us, event | category | flops | bytes accessed | tf_op | source)
XLA Modules:
  0.0 124.5 jit_solution(9104592738128043441)
XLA Ops:
  0.0 122.7 %shard_map.55 = bf16[8,64,256]{2,1,0:T(8,128)(2,1)} custom-call(bf16[512,256]{1,0:T(8,128)(2,1)} %bitcast.8, bf16[2,8,16,1024]{3,2,1,0:T(8,128)(2,1)} %bitcast.6, bf16[2,8,16,1024]{3,2,1,0:T(8,128)(2,1)} %bitcast.7, f32[2,1024]{1,0:T(2,128)} %bias_hbm.1, s32[128,128]{1,0:T(8,128)} %bitcast.9), custom_call_target="tpu_custom_call" | custom-call | tf_op jit(solution)/shard_map/pallas_call | solution.py:339
  122.7 1.8 %copy.6 = bf16[64,8,256]{2,1,0:T(8,128)(2,1)} copy(bf16[64,8,256]{2,0,1:T(8,128)(2,1)} %bitcast.5) | data formatting | bytes 524288 | tf_op jit(solution)/shard_map/transpose | solution.py:381

commit v6 on v5

--- a/solution.py
+++ b/solution.py
@@ -144,6 +144,8 @@
     x[m] = matmul(order, tokens_ref[...]).astype(jnp.bfloat16)
     for d in (2, 1, 0):
         input_copy(d, m).start()
+    for n in range(2):
+        tick(n)
 
     lanes = 128
     per_row = lanes // 4
@@ -163,7 +165,7 @@
     def rows_of(arr, i):
         return w.at[arr, pl.ds(i * 16, 16)]
 
-    @pl.loop(0, ITEMS)
+    @pl.loop(2, ITEMS)
     def _(n):
         tick(n)
 
@@ -199,12 +201,14 @@
             update(lambda k: proj[0, h, :, k * 256 : k * 256 + 256], states, layer, 0, h, first=True)
             send_state(states, layer, 0, h)
 
-    def step(states, layer, t, h):
+    def step(states, layer, t, h, between=None):
         arr = 2 * layer + 1
 
         state_copy(states, layer, t - 1, h, 0, mates[0]).wait_recv()
         near = jnp.concatenate([states[t - 1, h, here + i] for i in range(2)], axis=1)
         pre = proj[t, h] + matmul(near, w[arr, pl.ds(here * 16, 32)].reshape(512, 1024))
+        if between is not None:
+            between()
         for d in (1, 2):
             state_copy(states, layer, t - 1, h, d, mates[d]).wait_recv()
             far = states[t - 1, h, mates[d]]
@@ -233,8 +237,7 @@
     def _(t):
         p = t // 2
         n = 2 * ITEMS + 3 * (t - 1)
-        step(s0, 0, t, 0)
-        tick(n)
+        step(s0, 0, t, 0, between=lambda: tick(n))
         for h in range(1, PARTS):
             step(s0, 0, t, h)
         tick(n + 1)

time: 125 us -> 125 us (level)
  no operation moved by 1% of the time
where the time goes in v6:
time: 125 us
  Pallas kernels  123 us (98%)
  local copies, waits for them, and re-layouts  1.8 us (1%)
    pallas_call x1, Pallas kernels, local(): pl.pallas_call(kernel, out_shape=jax.ShapeDtypeStruct((steps, seqs, units...  123 us

profile of v6, /device:TPU:1, one launch (start us, length us, event | category | flops | bytes accessed | tf_op | source)
XLA Modules:
  0.0 124.5 jit_solution(1360316911895019549)
XLA Ops:
  0.0 122.7 %shard_map.55 = bf16[8,64,256]{2,1,0:T(8,128)(2,1)} custom-call(bf16[512,256]{1,0:T(8,128)(2,1)} %bitcast.8, bf16[2,8,16,1024]{3,2,1,0:T(8,128)(2,1)} %bitcast.6, bf16[2,8,16,1024]{3,2,1,0:T(8,128)(2,1)} %bitcast.7, f32[2,1024]{1,0:T(2,128)} %bias_hbm.1, s32[128,128]{1,0:T(8,128)} %bitcast.9), custom_call_target="tpu_custom_call" | custom-call | tf_op jit(solution)/shard_map/pallas_call | solution.py:342
  122.7 1.8 %copy.6 = bf16[64,8,256]{2,1,0:T(8,128)(2,1)} copy(bf16[64,8,256]{2,0,1:T(8,128)(2,1)} %bitcast.5) | data formatting | bytes 524288 | tf_op jit(solution)/shard_map/transpose | solution.py:384

commit v7 on v6

--- a/solution.py
+++ b/solution.py
@@ -312,18 +312,16 @@
     def _(p):
         project_mixed(p)
 
-    for n in range(4 * ITEMS - DEPTH, 4 * ITEMS):
+    for n in range(4 * ITEMS - DEPTH, 4 * ITEMS - 1):
         tick(n, False)
+    project_mixed(steps // 2 - 1)
+    tick(4 * ITEMS - 1, False)
 
     @pl.loop(1, steps)
     def _(t):
         for h in range(PARTS):
             step(s1, 1, t, h)
         store(t - 1)
-
-        @pl.when(t == 1)
-        def _():
-            project_mixed(steps // 2 - 1)
 
     store(steps - 1)
 

time: 125 us -> 126 us (level)
    pallas_call x1, Pallas kernels: 123 us -> 124 us  [local(): pl.pallas_call(kernel, out_shape=jax.ShapeDtypeStruct((steps, seqs, units...]
where the time goes in v7:
time: 126 us
  Pallas kernels  124 us (98%)
  local copies, waits for them, and re-layouts  1.8 us (1%)
    pallas_call x1, Pallas kernels, local(): pl.pallas_call(kernel, out_shape=jax.ShapeDtypeStruct((steps, seqs, units...  124 us

profile of v7, /device:TPU:1, one launch (start us, length us, event | category | flops | bytes accessed | tf_op | source)
XLA Modules:
  0.0 126.1 jit_solution(14291617091700702236)
XLA Ops:
  0.0 124.3 %shard_map.55 = bf16[8,64,256]{2,1,0:T(8,128)(2,1)} custom-call(bf16[512,256]{1,0:T(8,128)(2,1)} %bitcast.8, bf16[2,8,16,1024]{3,2,1,0:T(8,128)(2,1)} %bitcast.6, bf16[2,8,16,1024]{3,2,1,0:T(8,128)(2,1)} %bitcast.7, f32[2,1024]{1,0:T(2,128)} %bias_hbm.1, s32[128,128]{1,0:T(8,128)} %bitcast.9), custom_call_target="tpu_custom_call" | custom-call | tf_op jit(solution)/shard_map/pallas_call | solution.py:340
  124.3 1.8 %copy.6 = bf16[64,8,256]{2,1,0:T(8,128)(2,1)} copy(bf16[64,8,256]{2,0,1:T(8,128)(2,1)} %bitcast.5) | data formatting | bytes 524288 | tf_op jit(solution)/shard_map/transpose | solution.py:382
